TPU v7x, 32 devices: a whole 2x2x4 slice. The times are simulated.
32 devices in a mesh: tx: 2 (over y), ty: 4 (over z), gz: 4 (over x, core).
Axes of the slice: x: 2, y: 2, z: 4, core: 2. Of those that a mesh axis runs over, the one named last changes fastest.
Arguments:
- tracer_in: float32 [100, 256, 256], P('gz', 'ty', 'tx'), may hold values from -6 to 6
- coef_h: float32 [3, 256, 256], P(None, 'ty', 'tx'), may hold values from 0.05 to 0.2
- coef_v: float32 [3, 100], replicated, may hold values from 0.3 to 1
- wet_levels: int32 [256, 256], P('ty', 'tx'), may hold values from 0 to 100
- column_inv: float32 [100, 100], replicated, may hold values from -0.1 to 1
- sec_cell: int32 [2048], P(('tx', 'ty')), may hold values from 0 to 8191
- sec_gate: int32 [2048], P(('tx', 'ty')), may hold values from 0 to 63
- sec_weight: float32 [2048], P(('tx', 'ty')), may hold values from -6 to 6
Outputs:
- tracer_out: float32 [100, 256, 256], P('gz', 'ty', 'tx')
- gate_flux: float32 [64, 100], P(('tx', 'ty'), 'gz')
Inputs may be any that keep to these rules, and one draw needn't show every extreme that they name: `sec_cell`: index of a cell within the tile of the slot.
All inputs are finite; a program needn't handle non-finite values.
Results may differ from a plain program's by a relative error of at most 0.00015.
Values sent between devices are 32-bit elements; how exact they have to be, the bound alone decides.
A program may use at most 64 MiB of HBM per device.

v0:
```python
import jax
import jax.numpy as jnp
from jax import lax
from jax.sharding import PartitionSpec as P

NSUB = 3
G_DEV = 8
HI = lax.Precision.HIGHEST


def extended(block, axis, dim, width):
    count = lax.axis_size(axis)
    forward = [(i, i + 1) for i in range(count - 1)]
    backward = [(target, source) for source, target in forward]
    low = lax.ppermute(
        lax.slice_in_dim(block, block.shape[dim] - width, None, axis=dim), axis, forward
    )
    high = lax.ppermute(lax.slice_in_dim(block, 0, width, axis=dim), axis, backward)
    return jnp.concatenate([low, block, high], axis=dim)


def diffuse(padded, coef_h, coef_v, wet_levels, level_ids):
    centre = padded[:, 1:-1, 1:-1]
    coef_x = coef_h[0][None] * coef_v[0][:, None, None]
    coef_y = coef_h[1][None] * coef_v[1][:, None, None]
    coef_s = coef_h[2][None] * coef_v[2][:, None, None]
    along_x = padded[:, 1:-1, 2:] - 2.0 * centre + padded[:, 1:-1, :-2]
    along_y = padded[:, 2:, 1:-1] - 2.0 * centre + padded[:, :-2, 1:-1]
    cross = padded[:, 2:, 2:] - padded[:, 2:, :-2] - padded[:, :-2, 2:] + padded[:, :-2, :-2]
    wet = (level_ids[:, None, None] < wet_levels[None]).astype(jnp.float32)
    return wet * (centre + coef_x * along_x + coef_y * along_y + 0.25 * coef_s * cross)


def substeps(field, coef_h, coef_v, wet_levels, level_ids):
    for ring in range(1, NSUB + 1):
        inner = coef_h[:, ring:-ring, ring:-ring]
        field = diffuse(field, inner, coef_v, wet_levels[ring:-ring, ring:-ring], level_ids)
    return field


def vertical(field, column_inv, wet_levels, level_ids):
    levels = column_inv.shape[0]
    flat = field.reshape(levels, -1)
    solved = jnp.dot(column_inv.T, flat, precision=HI).reshape(field.shape)
    wet = (level_ids[:, None, None] < wet_levels[None]).astype(jnp.float32)
    return wet * solved


def per_device(tracer_in, coef_h, coef_v, wet_levels, column_inv, sec_cell, sec_gate, sec_weight):
    depth_count = lax.axis_size("gz")
    depth_index = lax.axis_index("gz")
    tiles = lax.axis_size(("tx", "ty"))
    local_levels, rows, width = tracer_in.shape
    levels = local_levels * depth_count
    col_rows = rows // depth_count
    level_ids = depth_index * local_levels + jnp.arange(local_levels, dtype=jnp.int32)
    all_ids = jnp.arange(levels, dtype=jnp.int32)
    coef_depth = lax.dynamic_slice_in_dim(coef_v, depth_index * local_levels, local_levels, 1)
    row_start = depth_index * col_rows
    gate_ids = jnp.arange(G_DEV * tiles, dtype=jnp.int32)
    gate_hot = jnp.where(gate_ids[:, None] == sec_gate[None, :], sec_weight[None, :], 0.0)
    cells = row_start * width + jnp.arange(col_rows * width, dtype=jnp.int32)
    cell_hot = (sec_cell[:, None] == cells[None, :]).astype(jnp.float32)
    gate_cells = jnp.dot(gate_hot, cell_hot, precision=HI)
    rim = 2 * NSUB
    wet_depth = (level_ids[:, None, None] < wet_levels[None]).astype(jnp.float32)
    packed = jnp.concatenate(
        [wet_depth * tracer_in, coef_h, wet_levels[None].astype(jnp.float32)], axis=0
    )
    packed = extended(extended(packed, "tx", 2, rim), "ty", 1, rim)
    field = packed[:local_levels]
    coef_h = packed[local_levels:-1]
    wet_levels = packed[-1].astype(jnp.int32)
    field = substeps(field, coef_h, coef_depth, wet_levels, level_ids)
    tall = col_rows + 2 * NSUB
    sent = jnp.stack(
        [field[:, part * col_rows : part * col_rows + tall, :] for part in range(depth_count)]
    )
    sent = sent.reshape(depth_count, local_levels, -1)
    field = lax.all_to_all(sent, "gz", split_axis=0, concat_axis=0, tiled=True)
    field = field.reshape(levels, tall, -1)
    coef_h = lax.dynamic_slice_in_dim(coef_h, row_start + NSUB, tall, 1)[:, :, NSUB:-NSUB]
    wet_levels = lax.dynamic_slice_in_dim(wet_levels, row_start + NSUB, tall, 0)[:, NSUB:-NSUB]
    field = vertical(field, column_inv, wet_levels, all_ids)
    total = field[:, NSUB:-NSUB, NSUB:-NSUB]
    field = substeps(field, coef_h, coef_v, wet_levels, all_ids)
    field = vertical(field, column_inv, wet_levels[NSUB:-NSUB, NSUB:-NSUB], all_ids)
    total = total + field
    out = lax.all_to_all(field, "gz", split_axis=0, concat_axis=1, tiled=True)
    flux = lax.dot_general(
        gate_cells, total.reshape(levels, -1), (((1,), (1,)), ((), ())), precision=HI
    )
    flux = flux.reshape(tiles, G_DEV, depth_count, local_levels).transpose(0, 2, 1, 3)
    flux = flux.reshape(tiles * depth_count, G_DEV * local_levels)
    flux = lax.all_to_all(flux, ("tx", "ty", "gz"), split_axis=0, concat_axis=0, tiled=True)
    flux = jnp.sum(flux, axis=0).reshape(G_DEV, local_levels)
    return (out, flux)


def solution(mesh):
    in_specs = (
        P("gz", "ty", "tx"),
        P(None, "ty", "tx"),
        P(),
        P("ty", "tx"),
        P(),
        P(("tx", "ty")),
        P(("tx", "ty")),
        P(("tx", "ty")),
    )
    out_specs = (P("gz", "ty", "tx"), P(("tx", "ty"), "gz"))
    return jax.shard_map(
        per_device, mesh=mesh, in_specs=in_specs, out_specs=out_specs, check_vma=False
    )
```

profile of v0, /device:TPU:0, one launch (start us, length us, event | category | flops | bytes accessed | tf_op | source)
XLA Modules:
  0.0 136.1 jit_solution(9009648317094486944)
XLA Ops:
  4.4 4.9 %collective-permute-start = (f32[29,64,6]{1,0,2:T(8,128)S(1)}, f32[29,64,6]{1,0,2:T(8,128)S(1)}, u32[]{:S(2)}, u32[]{:S(2)}) collective-permute-start(f32[29,64,6]{1,0,2:T(8,128)S(1)} %copy.47), channel_id=1, source_target_pairs={{0,16},{1,17},{2,18},{3,19},{4,20},{5,21},{6,22},{7,23},{8,24},{9,... | collective-permute-start | bytes 133640 | tf_op jit(solution)/shard_map/ppermute | solution.py:15
  11.9 4.3 %collective-permute-done.1 = f32[29,64,6]{1,0,2:T(8,128)S(1)} collective-permute-done((f32[29,64,6]{1,0,2:T(8,128)S(1)}, f32[29,64,6]{1,0,2:T(8,128)S(1)}, u32[]{:S(2)}, u32[]{:S(2)}) %collective-permute-start.1) | collective-permute-done | bytes 44576 | tf_op jit(solution)/shard_map/ppermute | solution.py:18
  17.7 3.5 %collective-permute-start.2 = (f32[29,6,140]{2,1,0:T(8,128)}, f32[29,6,140]{2,1,0:T(8,128)S(1)}, u32[]{:S(2)}, u32[]{:S(2)}) collective-permute-start(f32[29,6,140]{2,1,0:T(8,128)} %get-tuple-element.10), channel_id=1, source_target_pairs={{0,4},{4,8},{8,12},{1,5},{5,9},{9,13},{2,6},{6,10},{10,14},{3,7},{... | collective-permute-start | bytes 292328 | tf_op jit(solution)/shard_map/ppermute | solution.py:15
  22.5 2.6 %collective-permute-done.2 = f32[29,6,140]{2,1,0:T(8,128)S(1)} collective-permute-done((f32[29,6,140]{2,1,0:T(8,128)}, f32[29,6,140]{2,1,0:T(8,128)S(1)}, u32[]{:S(2)}, u32[]{:S(2)}) %collective-permute-start.2) | collective-permute-done | bytes 97472 | tf_op jit(solution)/shard_map/ppermute | solution.py:15
  25.1 4.3 %collective-permute-done.3 = f32[29,6,140]{2,1,0:T(8,128)S(1)} collective-permute-done((f32[29,6,140]{2,1,0:T(8,128)}, f32[29,6,140]{2,1,0:T(8,128)S(1)}, u32[]{:S(2)}, u32[]{:S(2)}) %collective-permute-start.3) | collective-permute-done | bytes 97472 | tf_op jit(solution)/shard_map/ppermute | solution.py:18
  39.1 2.6 %pad_maximum_fusion = f32[29,76,140]{2,1,0:T(8,128)S(1)} fusion(f32[29,6,140]{2,1,0:T(8,128)} %copy-done.5, f32[29,64,6]{2,1,0:T(8,128)} %copy-done.3, f32[1,64,128]{2,1,0:T(8,128)S(1)} %convert_bitcast_fusion, f32[3,64,128]{2,1,0:T(8,128)S(1)} %copy-done.8, f32[25,64,128]{2,1,0:T(8,128)S(1)} %compare_select_fusion, f32[29,64,6]{2,1,0:T(8,128)} %copy-done.1, ...), kind=kLoop, calls=%fused_computation.2 | loop fusion | flops 1851360 | bytes 2468480 | tf_op jit(solution)/shard_map/concatenate | solution.py:19
  41.7 3.7 %fusion.3 = f32[25,74,138]{2,1,0:T(8,128)S(1)} fusion(f32[29,76,140]{2,1,0:T(8,128)S(1)} %pad_maximum_fusion, f32[25]{0:T(128)S(1)} %get-tuple-element.31, f32[74,138]{1,0:T(8,128)S(1)} %get-tuple-element.9, f32[25]{0:T(128)S(1)} %get-tuple-element.32, f32[74,138]{1,0:T(8,128)S(1)} %maximum_bitcast_fusion.1, f32[25]{0:T(128)S(1)} %get-tuple-element.30, ...), kind=kLoop, calls=%fused_computation.8 | loop fusion | flops 5106000 | bytes 10375792 | tf_op jit(solution)/shard_map/mul | solution.py:31
  46.4 3.3 %fusion.17 = f32[25,72,136]{2,1,0:T(8,128)S(1)} fusion(f32[25,74,138]{2,1,0:T(8,128)S(1)} %fusion.3, f32[25]{0:T(128)S(1)} %get-tuple-element.31, f32[72,136]{1,0:T(8,128)S(1)} %get-tuple-element.7, f32[25]{0:T(128)S(1)} %get-tuple-element.32, f32[72,136]{1,0:T(8,128)S(1)} %maximum_bitcast_fusion.7, f32[25]{0:T(128)S(1)} %get-tuple-element.30, ...), kind=kLoop, calls=%fused_computation.36 | loop fusion | flops 4896000 | bytes 9949072 | tf_op jit(solution)/shard_map/mul | solution.py:31
  50.7 3.3 %fusion.10 = f32[25,70,134]{2,1,0:T(8,128)S(1)} fusion(f32[25,72,136]{2,1,0:T(8,128)S(1)} %fusion.17, f32[25]{0:T(128)S(1)} %get-tuple-element.31, f32[70,134]{1,0:T(8,128)S(1)} %get-tuple-element.5, f32[25]{0:T(128)S(1)} %get-tuple-element.32, f32[70,134]{1,0:T(8,128)S(1)} %maximum_bitcast_fusion.4, f32[25]{0:T(128)S(1)} %get-tuple-element.30, ...), kind=kLoop, calls=%fused_computation.22 | loop fusion | flops 4690000 | bytes 9530480 | tf_op jit(solution)/shard_map/mul | solution.py:31
  56.7 2.1 %stack.16 = f32[1,25,2948]{2,1,0:T(8,128)} reshape(f32[25,22,134]{2,1,0:T(8,128)} %get-tuple-element.15) | data formatting | bytes 589600 | tf_op jit(solution)/shard_map/stack | solution.py:76
  58.7 2.1 %stack.17 = f32[1,25,2948]{2,1,0:T(8,128)} reshape(f32[25,22,134]{2,1,0:T(8,128)} %get-tuple-element.14) | data formatting | bytes 589600 | tf_op jit(solution)/shard_map/stack | solution.py:76
  61.8 2.6 %pad_maximum_fusion.1 = f32[4,25,2948]{2,1,0:T(8,128)} fusion(f32[1,25,2948]{2,1,0:T(8,128)} %stack.18, f32[1,25,2948]{2,1,0:T(8,128)} %stack.17, f32[1,25,2948]{2,1,0:T(8,128)} %stack.16, f32[1,25,2948]{2,1,0:T(8,128)S(1)} %stack.15), kind=kLoop, calls=%fused_computation.47 | loop fusion | flops 884400 | bytes 2358400 | tf_op jit(solution)/shard_map/stack | solution.py:76
  64.4 4.7 %all-to-all-start = ((f32[4,25,2948]{2,1,0:T(8,128)}), f32[4,25,2948]{2,1,0:T(8,128)}, u32[]{:S(2)}, u32[]{:S(2)}) async-start(f32[4,25,2948]{2,1,0:T(8,128)} %pad_maximum_fusion.1), calls=%async_computation | async-start | bytes 3145728 | tf_op jit(solution)/shard_map/all_to_all | solution.py:80
  69.1 1.7 %convolution_bitcast_fusion.2 = f32[8,8,2048,1]{2,1,3,0:T(8,128)} fusion(s32[2048]{0:T(1024)S(1)} %iota_add_fusion, s32[256]{0:T(256)S(1)} %copy-done.13, f32[256]{0:T(256)S(1)} %copy-done.14, s32[256]{0:T(256)S(1)} %copy-done.15), kind=kOutput, calls=%fused_computation.3 | convolution fusion | flops 403210240 | bytes 535552 | tf_op jit(solution)/shard_map/dot_general | solution.py:64
  72.2 16.8 %all-to-all-done = f32[4,25,2948]{2,1,0:T(8,128)} async-done(((f32[4,25,2948]{2,1,0:T(8,128)}), f32[4,25,2948]{2,1,0:T(8,128)}, u32[]{:S(2)}, u32[]{:S(2)}) %all-to-all-start) | async-done | bytes 1179232 | tf_op jit(solution)/shard_map/all_to_all | solution.py:80
  93.1 1.9 %fusion.25 = f32[100,20,132]{0,2,1:T(8,128)S(1)} fusion(f32[100,22,134]{0,2,1:T(8,128)S(1)} %fusion.22, f32[100]{0:T(128)S(1)} %get-tuple-element.28, f32[20,132]{1,0:T(8,128)S(1)} %get-tuple-element.25, f32[100]{0:T(128)S(1)} %get-tuple-element.29, f32[20,132]{1,0:T(8,128)S(1)} %get-tuple-element.26, f32[100]{0:T(128)S(1)} %get-tuple-element.27, ...), kind=kLoop, calls=%fused_computation.53 | loop fusion | flops 5280000 | bytes 10603440 | tf_op jit(solution)/shard_map/mul | solution.py:31
  95.0 1.8 %fusion.32 = f32[100,18,130]{0,2,1:T(8,128)S(1)} fusion(f32[100,20,132]{0,2,1:T(8,128)S(1)} %fusion.25, f32[100]{0:T(128)S(1)} %get-tuple-element.28, f32[18,130]{1,0:T(8,128)S(1)} %get-tuple-element.22, f32[100]{0:T(128)S(1)} %get-tuple-element.29, f32[18,130]{1,0:T(8,128)S(1)} %get-tuple-element.23, f32[100]{0:T(128)S(1)} %get-tuple-element.27, ...), kind=kLoop, calls=%fused_computation.68 | loop fusion | flops 4680000 | bytes 9398640 | tf_op jit(solution)/shard_map/mul | solution.py:31
  100.8 2.3 %slice_add_fusion.15 = (f32[100,16,128]{0,2,1:T(8,128)}, f32[100,16,128]{0,2,1:T(8,128)S(1)}) fusion(f32[100,22,134]{0,2,1:T(8,128)S(1)} %fusion.22, f32[100,16,128]{0,2,1:T(8,128)} %bitcast.81, s32[16,128]{1,0:T(8,128)S(1)} %slice.443), kind=kLoop, calls=%fused_computation.81 | loop fusion | flops 614400 | bytes 3284992 | tf_op jit(solution)/shard_map/add | solution.py:88
  103.1 1.7 %copy.71 = f32[100,16,128]{2,1,0:T(8,128)S(1)} copy(f32[100,16,128]{0,2,1:T(8,128)} %get-tuple-element.2) | data formatting | bytes 1638400 | tf_op jit(solution)/shard_map/add | solution.py:88
  104.9 3.7 %convolution_bitcast_fusion.3 = f32[8,4,8,25]{3,2,1,0:T(8,128)S(1)} fusion(f32[8,8,2048,1]{2,1,3,0:T(8,128)} %convolution_bitcast_fusion.2, f32[4,25,2048,1]{2,1,0,3:T(8,128)S(1)} %reshape.67), kind=kOutput, calls=%fused_computation.80 | convolution fusion | flops 157286400 | bytes 1369088 | tf_op jit(solution)/shard_map/dot_general | solution.py:90
  109.4 2.9 %all-to-all-start.2 = ((f32[32,1,200]{2,1,0:T(1,128)}), f32[32,1,200]{2,1,0:T(1,128)S(1)}, u32[]{:S(2)}, u32[]{:S(2)}) async-start(f32[32,1,200]{2,1,0:T(1,128)} %all_to_all.29), calls=%async_computation.2 | async-start | bytes 65536 | tf_op jit(solution)/shard_map/all_to_all | solution.py:95
  113.6 5.9 %all-to-all-done.2 = f32[32,1,200]{2,1,0:T(1,128)S(1)} async-done(((f32[32,1,200]{2,1,0:T(1,128)}), f32[32,1,200]{2,1,0:T(1,128)S(1)}, u32[]{:S(2)}, u32[]{:S(2)}) %all-to-all-start.2) | async-done | bytes 25632 | tf_op jit(solution)/shard_map/all_to_all | solution.py:95
  119.6 3.5 %all-to-all-start.1 = ((f32[100,16,128]{2,1,0:T(8,128)}), f32[100,16,128]{2,1,0:T(8,128)S(1)}, u32[]{:S(2)}, u32[]{:S(2)}) async-start(f32[100,16,128]{2,1,0:T(8,128)} %copy.69), calls=%async_computation.1 | async-start | bytes 1638400 | tf_op jit(solution)/shard_map/all_to_all | solution.py:89
  123.8 11.2 %all-to-all-done.1 = f32[100,16,128]{2,1,0:T(8,128)S(1)} async-done(((f32[100,16,128]{2,1,0:T(8,128)}), f32[100,16,128]{2,1,0:T(8,128)S(1)}, u32[]{:S(2)}, u32[]{:S(2)}) %all-to-all-start.1) | async-done | bytes 819232 | tf_op jit(solution)/shard_map/all_to_all | solution.py:89
  (89 shorter events, 37.6 us)
Async XLA Ops:
  0.6 89.9 %copy-start = (f32[100,100]{1,0:T(8,128)S(1)}, f32[100,100]{1,0:T(8,128)}, u32[]{:S(2)}) copy-start(f32[100,100]{1,0:T(8,128)} %param.12) | copy-start | bytes 120004
  4.0 7.0 %copy-start.12 = (f32[3,100]{1,0:T(4,128)S(1)}, f32[3,100]{1,0:T(4,128)}, u32[]{:S(2)}) copy-start(f32[3,100]{1,0:T(4,128)} %param.10) | copy-start | bytes 3604
  4.0 12.6 %copy-start.7 = (f32[3,64,128]{2,1,0:T(8,128)S(1)}, f32[3,64,128]{2,1,0:T(8,128)}, u32[]{:S(2)}) copy-start(f32[3,64,128]{2,1,0:T(8,128)} %param.9) | copy-start | bytes 294916
  4.4 7.1 %collective-permute-start = (f32[29,64,6]{1,0,2:T(8,128)S(1)}, f32[29,64,6]{1,0,2:T(8,128)S(1)}, u32[]{:S(2)}, u32[]{:S(2)}) collective-permute-start(f32[29,64,6]{1,0,2:T(8,128)S(1)} %copy.47), channel_id=1, source_target_pairs={{0,16},{1,17},{2,18},{3,19},{4,20},{5,21},{6,22},{7,23},{8,24},{9,... | collective-permute-start | bytes 133640 | tf_op jit(solution)/shard_map/ppermute | solution.py:15
  9.7 6.5 %collective-permute-start.1 = (f32[29,64,6]{1,0,2:T(8,128)S(1)}, f32[29,64,6]{1,0,2:T(8,128)S(1)}, u32[]{:S(2)}, u32[]{:S(2)}) collective-permute-start(f32[29,64,6]{1,0,2:T(8,128)S(1)} %copy.48), channel_id=1, source_target_pairs={{16,0},{17,1},{18,2},{19,3},{20,4},{21,5},{22,6},{23,7},{24,8},{25... | collective-permute-start | bytes 133640 | tf_op jit(solution)/shard_map/ppermute | solution.py:18
  11.9 26.3 %copy-start.1 = (f32[29,64,6]{2,1,0:T(8,128)}, f32[29,64,6]{2,1,0:T(8,128)S(1)}, u32[]{:S(2)}) copy-start(f32[29,64,6]{2,1,0:T(8,128)S(1)} %copy.49) | copy-start | bytes 133636
  16.6 21.6 %copy-start.3 = (f32[29,64,6]{2,1,0:T(8,128)}, f32[29,64,6]{2,1,0:T(8,128)S(1)}, u32[]{:S(2)}) copy-start(f32[29,64,6]{2,1,0:T(8,128)S(1)} %copy.50) | copy-start | bytes 133636
  17.7 7.4 %collective-permute-start.2 = (f32[29,6,140]{2,1,0:T(8,128)}, f32[29,6,140]{2,1,0:T(8,128)S(1)}, u32[]{:S(2)}, u32[]{:S(2)}) collective-permute-start(f32[29,6,140]{2,1,0:T(8,128)} %get-tuple-element.10), channel_id=1, source_target_pairs={{0,4},{4,8},{8,12},{1,5},{5,9},{9,13},{2,6},{6,10},{10,14},{3,7},{... | collective-permute-start | bytes 292328 | tf_op jit(solution)/shard_map/ppermute | solution.py:15
  21.2 8.2 %collective-permute-start.3 = (f32[29,6,140]{2,1,0:T(8,128)}, f32[29,6,140]{2,1,0:T(8,128)S(1)}, u32[]{:S(2)}, u32[]{:S(2)}) collective-permute-start(f32[29,6,140]{2,1,0:T(8,128)} %get-tuple-element.11), channel_id=1, source_target_pairs={{4,0},{8,4},{12,8},{5,1},{9,5},{13,9},{6,2},{10,6},{14,10},{7,3},{... | collective-permute-start | bytes 292328 | tf_op jit(solution)/shard_map/ppermute | solution.py:18
  29.4 8.8 %copy-start.5 = (f32[29,6,140]{2,1,0:T(8,128)}, f32[29,6,140]{2,1,0:T(8,128)S(1)}, u32[]{:S(2)}) copy-start(f32[29,6,140]{2,1,0:T(8,128)S(1)} %collective-permute-done.3) | copy-start | bytes 292324
  38.2 0.9 copy-start.8
  39.1 2.6 %copy-start.9 = (s32[74,138]{1,0:T(8,128)S(1)}, s32[74,138]{1,0:T(8,128)}, u32[]{:S(2)}) copy-start(s32[74,138]{1,0:T(8,128)} %copy.54) | copy-start | bytes 122548
  41.7 3.7 %copy-start.2 = (f32[29,64,6]{2,1,0:T(8,128)S(1)}, f32[29,64,6]{2,1,0:T(8,128)}, u32[]{:S(2)}) copy-start(f32[29,64,6]{2,1,0:T(8,128)} %copy-done.1) | copy-start | bytes 133636
  41.7 3.7 %copy-start.4 = (f32[29,64,6]{2,1,0:T(8,128)S(1)}, f32[29,64,6]{2,1,0:T(8,128)}, u32[]{:S(2)}) copy-start(f32[29,64,6]{2,1,0:T(8,128)} %copy-done.3) | copy-start | bytes 133636
  41.7 3.7 %copy-start.6 = (f32[29,6,140]{2,1,0:T(8,128)S(1)}, f32[29,6,140]{2,1,0:T(8,128)}, u32[]{:S(2)}) copy-start(f32[29,6,140]{2,1,0:T(8,128)} %copy-done.5) | copy-start | bytes 292324
  45.5 0.9 copy-start.11
  49.8 0.9 copy-start.10
  64.4 4.7 %copy-start.13 = (s32[256]{0:T(256)S(1)}, s32[256]{0:T(256)}, u32[]{:S(2)}) copy-start(s32[256]{0:T(256)} %param.13) | copy-start | bytes 3076
  64.4 4.7 %copy-start.14 = (f32[256]{0:T(256)S(1)}, f32[256]{0:T(256)}, u32[]{:S(2)}) copy-start(f32[256]{0:T(256)} %param.15) | copy-start | bytes 3076
  64.4 4.7 %copy-start.15 = (s32[256]{0:T(256)S(1)}, s32[256]{0:T(256)}, u32[]{:S(2)}) copy-start(s32[256]{0:T(256)} %param.14) | copy-start | bytes 3076
  64.4 24.6 %all-to-all-start = ((f32[4,25,2948]{2,1,0:T(8,128)}), f32[4,25,2948]{2,1,0:T(8,128)}, u32[]{:S(2)}, u32[]{:S(2)}) async-start(f32[4,25,2948]{2,1,0:T(8,128)} %pad_maximum_fusion.1), calls=%async_computation | async-start | bytes 3145728 | tf_op jit(solution)/shard_map/all_to_all | solution.py:80
  109.4 10.2 %all-to-all-start.2 = ((f32[32,1,200]{2,1,0:T(1,128)}), f32[32,1,200]{2,1,0:T(1,128)S(1)}, u32[]{:S(2)}, u32[]{:S(2)}) async-start(f32[32,1,200]{2,1,0:T(1,128)} %all_to_all.29), calls=%async_computation.2 | async-start | bytes 65536 | tf_op jit(solution)/shard_map/all_to_all | solution.py:95
  119.6 15.5 %all-to-all-start.1 = ((f32[100,16,128]{2,1,0:T(8,128)}), f32[100,16,128]{2,1,0:T(8,128)S(1)}, u32[]{:S(2)}, u32[]{:S(2)}) async-start(f32[100,16,128]{2,1,0:T(8,128)} %copy.69), calls=%async_computation.1 | async-start | bytes 1638400 | tf_op jit(solution)/shard_map/all_to_all | solution.py:89
where the time goes:
time: 137 us; the launch traced here: 136 us
  waiting for transfers between devices  45.6 us (33%)
  local copies, waits for them, and re-layouts  30.3 us (22%)
  other arithmetic  29.2 us (21%)
  starting transfers between devices  22 us (16%)
  matrix products  7.83 us (6%)
    all_to_all x1, waiting for transfers between devices, per_device(): field = lax.all_to_all(sent, 'gz', split_axis=0, concat_axis=0, tiled=True)  16.8 us
    mul x6, other arithmetic, diffuse(): wet * (centre + coef_x * along_x + coef_y * along_y + 0.25 * coef_s * cross)  15.5 us
    all_to_all x1, waiting for transfers between devices, per_device(): out = lax.all_to_all(field, 'gz', split_axis=0, concat_axis=1, tiled=True)  11.2 us
    ppermute x2, waiting for transfers between devices, extended(): lax.ppermute(lax.slice_in_dim(block, 0, width, axis=dim), axis, backward)  8.61 us
    ppermute x2, starting transfers between devices, extended(): lax.ppermute(lax.slice_in_dim(block, block.shape[dim] - width, None, axis...  8.36 us
    slice x8, local copies, waits for them, and re-layouts, substeps(): wet_levels[ring:-ring, ring:-ring]  7.11 us
    another operation x4, local copies, waits for them, and re-layouts, per_device(): jnp.stack([field[:, part * col_rows:part * col_rows + tall, :] for part i...  6.45 us
    all_to_all x1, waiting for transfers between devices, per_device(): lax.all_to_all(flux, ('tx', 'ty', 'gz'), split_axis=0, concat_axis=0, til...  5.94 us
  transfers between devices with their start and end apart: 7, of which 7 were waited for; matrix products, arithmetic and copies ran while one was open for 4% of the time, Pallas kernels for 0%

commit v1 on v0

--- a/solution.py
+++ b/solution.py
@@ -6,6 +6,28 @@
 NSUB = 3
 G_DEV = 8
 HI = lax.Precision.HIGHEST
+
+
+def in_blocks(x, dim, size):
+    before, after = (x.shape[:dim], x.shape[dim + 1 :])
+    return jnp.moveaxis(x.reshape(*before, size, -1, *after), dim, 0)
+
+
+def in_order(pieces, dim):
+    pieces = jnp.moveaxis(pieces, 0, dim)
+    shape = pieces.shape
+    return pieces.reshape(*shape[:dim], shape[dim] * shape[dim + 1], *shape[dim + 2 :])
+
+
+def swapped_with_each(x, axis, split_dim, concat_dim):
+    peers, position = (lax.axis_size(axis), lax.axis_index(axis))
+    blocks = in_blocks(x, split_dim, peers)
+    gathered = [blocks[position]]
+    for step in range(1, peers):
+        sent = blocks[position ^ step]
+        gathered.append(lax.ppermute(sent, axis, [(i, i ^ step) for i in range(peers)]))
+    blocks = jnp.stack(gathered)[position ^ jnp.arange(peers)]
+    return in_order(blocks, concat_dim)
 
 
 def extended(block, axis, dim, width):
@@ -77,7 +99,7 @@
         [field[:, part * col_rows : part * col_rows + tall, :] for part in range(depth_count)]
     )
     sent = sent.reshape(depth_count, local_levels, -1)
-    field = lax.all_to_all(sent, "gz", split_axis=0, concat_axis=0, tiled=True)
+    field = swapped_with_each(sent, "gz", 0, 0)
     field = field.reshape(levels, tall, -1)
     coef_h = lax.dynamic_slice_in_dim(coef_h, row_start + NSUB, tall, 1)[:, :, NSUB:-NSUB]
     wet_levels = lax.dynamic_slice_in_dim(wet_levels, row_start + NSUB, tall, 0)[:, NSUB:-NSUB]

time: 137 us -> 121 us (0.88)
  local copies, waits for them, and re-layouts: 30.3 us -> 23.9 us
  other arithmetic: 29.2 us -> 24.4 us
  waiting for transfers between devices: 45.6 us -> 41.5 us
    ppermute x0 -> x3, waiting for transfers between devices: none -> 17.7 us  [swapped_with_each(): lax.ppermute(sent, axis, [(i, i ^ step) for i in range(peers)])]
    all_to_all x1 -> x0, waiting for transfers between devices: 16.8 us -> none  [per_device(): field = lax.all_to_all(sent, 'gz', split_axis=0, concat_axis=0, tiled=True)]
    another operation x4 -> x5, local copies, waits for them, and re-layouts: 6.45 us -> 1.09 us  [per_device(): jnp.stack([field[:, part * col_rows:part * col_rows + tall, :] for part i...]
    all_to_all x1 -> x0, starting transfers between devices: 4.65 us -> none  [per_device(): field = lax.all_to_all(sent, 'gz', split_axis=0, concat_axis=0, tiled=True)]
    ppermute x2, waiting for transfers between devices: 8.61 us -> 4.13 us  [extended(): lax.ppermute(lax.slice_in_dim(block, 0, width, axis=dim), axis, backward)]
    another operation x1, other arithmetic: 2.58 us -> 0.12 us  [swapped_with_each(): blocks = jnp.stack(gathered)[position ^ jnp.arange(peers)]]
    ppermute x0 -> x3, starting transfers between devices: none -> 1.92 us  [swapped_with_each(): lax.ppermute(sent, axis, [(i, i ^ step) for i in range(peers)])]
    concatenate x1, other arithmetic: 2.55 us -> 0.93 us  [extended(): return jnp.concatenate([low, block, high], axis=dim)]
  transfers between devices with their start and end apart: 7 -> 9, of which waited for: 7 -> 6; matrix products, arithmetic and copies ran while one was open for 4% -> 6% of each run, Pallas kernels for 0% -> 0%
where the time goes in v1:
time: 121 us; the launch traced here: 120 us
  waiting for transfers between devices  41.5 us (34%)
  other arithmetic  24.4 us (20%)
  local copies, waits for them, and re-layouts  23.9 us (20%)
  starting transfers between devices  20.9 us (17%)
  matrix products  7.83 us (6%)
    ppermute x3, waiting for transfers between devices, swapped_with_each(): lax.ppermute(sent, axis, [(i, i ^ step) for i in range(peers)])  17.7 us
    mul x6, other arithmetic, diffuse(): wet * (centre + coef_x * along_x + coef_y * along_y + 0.25 * coef_s * cross)  15.7 us
    all_to_all x1, waiting for transfers between devices, per_device(): out = lax.all_to_all(field, 'gz', split_axis=0, concat_axis=1, tiled=True)  11.2 us
    ppermute x2, starting transfers between devices, extended(): lax.ppermute(lax.slice_in_dim(block, block.shape[dim] - width, None, axis...  9.49 us
    all_to_all x1, waiting for transfers between devices, per_device(): lax.all_to_all(flux, ('tx', 'ty', 'gz'), split_axis=0, concat_axis=0, til...  5.94 us
    slice x8, local copies, waits for them, and re-layouts, substeps(): wet_levels[ring:-ring, ring:-ring]  5.54 us
    ppermute x2, waiting for transfers between devices, extended(): lax.ppermute(lax.slice_in_dim(block, 0, width, axis=dim), axis, backward)  4.13 us
    dot_general x1, matrix products, per_device(): lax.dot_general(gate_cells, total.reshape(levels, -1), (((1,), (1,)), (()...  3.75 us
  transfers between devices with their start and end apart: 9, of which 6 were waited for; matrix products, arithmetic and copies ran while one was open for 6% of the time, Pallas kernels for 0%

profile of v1, /device:TPU:0, one launch (start us, length us, event | category | flops | bytes accessed | tf_op | source)
XLA Modules:
  0.0 119.7 jit_solution(14814619938706143772)
XLA Ops:
  6.1 4.9 %collective-permute-start = (f32[29,64,6]{1,0,2:T(8,128)S(1)}, f32[29,64,6]{1,0,2:T(8,128)S(1)}, u32[]{:S(2)}, u32[]{:S(2)}) collective-permute-start(f32[29,64,6]{1,0,2:T(8,128)S(1)} %copy.47), channel_id=1, source_target_pairs={{0,16},{1,17},{2,18},{3,19},{4,20},{5,21},{6,22},{7,23},{8,24},{9,... | collective-permute-start | bytes 133640 | tf_op jit(solution)/shard_map/ppermute | solution.py:37
  12.3 1.7 %convolution_bitcast_fusion.2 = f32[8,8,2048,1]{2,1,3,0:T(8,128)} fusion(s32[2048]{0:T(1024)S(1)} %iota_add_fusion, s32[256]{0:T(256)S(1)} %copy-done.13, f32[256]{0:T(256)S(1)} %copy-done.14, s32[256]{0:T(256)S(1)} %copy-done.15), kind=kOutput, calls=%fused_computation.4 | convolution fusion | flops 403210240 | bytes 535552 | tf_op jit(solution)/shard_map/dot_general | solution.py:86
  15.1 4.6 %collective-permute-start.2 = (f32[29,6,140]{2,1,0:T(8,128)S(1)}, f32[29,6,140]{2,1,0:T(8,128)S(1)}, u32[]{:S(2)}, u32[]{:S(2)}) collective-permute-start(f32[29,6,140]{2,1,0:T(8,128)S(1)} %get-tuple-element.10), channel_id=1, source_target_pairs={{0,4},{4,8},{8,12},{1,5},{5,9},{9,13},{2,6},{6,10},{10,14},{3,7},{... | collective-permute-start | bytes 292328 | tf_op jit(solution)/shard_map/ppermute | solution.py:37
  19.7 1.3 %collective-permute-start.3 = (f32[29,6,140]{2,1,0:T(8,128)S(1)}, f32[29,6,140]{2,1,0:T(8,128)S(1)}, u32[]{:S(2)}, u32[]{:S(2)}) collective-permute-start(f32[29,6,140]{2,1,0:T(8,128)S(1)} %get-tuple-element.11), channel_id=1, source_target_pairs={{4,0},{8,4},{12,8},{5,1},{9,5},{13,9},{6,2},{10,6},{14,10},{7,3},{... | collective-permute-start | bytes 292328 | tf_op jit(solution)/shard_map/ppermute | solution.py:40
  21.6 2.5 %collective-permute-done.2 = f32[29,6,140]{2,1,0:T(8,128)S(1)} collective-permute-done((f32[29,6,140]{2,1,0:T(8,128)S(1)}, f32[29,6,140]{2,1,0:T(8,128)S(1)}, u32[]{:S(2)}, u32[]{:S(2)}) %collective-permute-start.2) | collective-permute-done | bytes 97472 | tf_op jit(solution)/shard_map/ppermute | solution.py:37
  24.1 4.1 %collective-permute-done.3 = f32[29,6,140]{2,1,0:T(8,128)S(1)} collective-permute-done((f32[29,6,140]{2,1,0:T(8,128)S(1)}, f32[29,6,140]{2,1,0:T(8,128)S(1)}, u32[]{:S(2)}, u32[]{:S(2)}) %collective-permute-start.3) | collective-permute-done | bytes 97472 | tf_op jit(solution)/shard_map/ppermute | solution.py:40
  38.7 3.6 %fusion.3 = f32[25,74,138]{2,1,0:T(8,128)S(1)} fusion(f32[29,76,140]{2,1,0:T(8,128)S(1)} %pad_maximum_fusion, f32[25]{0:T(128)S(1)} %copy-done.10, f32[74,138]{1,0:T(8,128)S(1)} %get-tuple-element.9, f32[25]{0:T(128)S(1)} %copy-done.11, f32[74,138]{1,0:T(8,128)S(1)} %maximum_bitcast_fusion.2, f32[25]{0:T(128)S(1)} %copy-done.9, ...), kind=kLoop, calls=%fused_computation.9 | loop fusion | flops 5106000 | bytes 10375792 | tf_op jit(solution)/shard_map/mul | solution.py:53
  43.4 3.3 %fusion.17 = f32[25,72,136]{2,1,0:T(8,128)S(1)} fusion(f32[25,74,138]{2,1,0:T(8,128)S(1)} %fusion.3, f32[25]{0:T(128)S(1)} %copy-done.10, f32[72,136]{1,0:T(8,128)S(1)} %get-tuple-element.7, f32[25]{0:T(128)S(1)} %copy-done.11, f32[72,136]{1,0:T(8,128)S(1)} %maximum_bitcast_fusion.8, f32[25]{0:T(128)S(1)} %copy-done.9, f32[72,136]{1,0:T(8,128)S(1)} %get-tuple-element.6, ...), kind=kLoop, calls=%fused_computation.37 | loop fusion | flops 4896000 | bytes 9949072 | tf_op jit(solution)/shard_map/mul | solution.py:53
  47.0 3.3 %fusion.10 = f32[25,70,134]{2,1,0:T(8,128)S(1)} fusion(f32[25,72,136]{2,1,0:T(8,128)S(1)} %fusion.17, f32[25]{0:T(128)S(1)} %copy-done.10, f32[70,134]{1,0:T(8,128)S(1)} %get-tuple-element.5, f32[25]{0:T(128)S(1)} %copy-done.11, f32[70,134]{1,0:T(8,128)S(1)} %maximum_bitcast_fusion.5, f32[25]{0:T(128)S(1)} %copy-done.9, f32[70,134]{1,0:T(8,128)S(1)} %get-tuple-element.4, ...), kind=kLoop, calls=%fused_computation.23 | loop fusion | flops 4690000 | bytes 9530480 | tf_op jit(solution)/shard_map/mul | solution.py:53
  51.9 1.6 %collective-permute-start.5 = (f32[1,25,2948]{2,1,0:T(8,128)S(1)}, f32[1,25,2948]{2,1,0:T(8,128)S(1)}, u32[]{:S(2)}, u32[]{:S(2)}) collective-permute-start(f32[1,25,2948]{2,1,0:T(8,128)S(1)} %get-tuple-element.18), channel_id=1, source_target_pairs={{0,2},{1,3},{2,0},{3,1},{4,6},{5,7},{6,4},{7,5},{8,10},{9,11},{10,... | collective-permute-start | bytes 884408 | tf_op jit(solution)/shard_map/ppermute | solution.py:28
  54.1 9.2 %collective-permute-done.6 = f32[1,25,2948]{2,1,0:T(8,128)S(1)} collective-permute-done((f32[1,25,2948]{2,1,0:T(8,128)S(1)}, f32[1,25,2948]{2,1,0:T(8,128)S(1)}, u32[]{:S(2)}, u32[]{:S(2)}) %collective-permute-start.6) | collective-permute-done | bytes 294832 | tf_op jit(solution)/shard_map/ppermute | solution.py:28
  63.3 8.5 %collective-permute-done.5 = f32[1,25,2948]{2,1,0:T(8,128)S(1)} collective-permute-done((f32[1,25,2948]{2,1,0:T(8,128)S(1)}, f32[1,25,2948]{2,1,0:T(8,128)S(1)}, u32[]{:S(2)}, u32[]{:S(2)}) %collective-permute-start.5) | collective-permute-done | bytes 294832 | tf_op jit(solution)/shard_map/ppermute | solution.py:28
  76.1 1.9 %fusion.25 = f32[100,20,132]{0,2,1:T(8,128)S(1)} fusion(f32[100,22,134]{0,2,1:T(8,128)S(1)} %fusion.22, f32[100]{0:T(128)S(1)} %get-tuple-element.32, f32[20,132]{1,0:T(8,128)S(1)} %get-tuple-element.29, f32[100]{0:T(128)S(1)} %copy-done.8, f32[20,132]{1,0:T(8,128)S(1)} %get-tuple-element.30, f32[100]{0:T(128)S(1)} %get-tuple-element.31, ...), kind=kLoop, calls=%fused_computation.54 | loop fusion | flops 5280000 | bytes 10603440 | tf_op jit(solution)/shard_map/mul | solution.py:53
  78.0 1.8 %fusion.32 = f32[100,18,130]{0,2,1:T(8,128)S(1)} fusion(f32[100,20,132]{0,2,1:T(8,128)S(1)} %fusion.25, f32[100]{0:T(128)S(1)} %get-tuple-element.32, f32[18,130]{1,0:T(8,128)S(1)} %get-tuple-element.26, f32[100]{0:T(128)S(1)} %copy-done.8, f32[18,130]{1,0:T(8,128)S(1)} %get-tuple-element.27, f32[100]{0:T(128)S(1)} %get-tuple-element.31, ...), kind=kLoop, calls=%fused_computation.69 | loop fusion | flops 4680000 | bytes 9398640 | tf_op jit(solution)/shard_map/mul | solution.py:53
  79.9 1.7 %fusion.39 = f32[100,16,128]{0,2,1:T(8,128)S(1)} fusion(f32[100,18,130]{0,2,1:T(8,128)S(1)} %fusion.32, f32[100]{0:T(128)S(1)} %get-tuple-element.32, f32[16,128]{1,0:T(8,128)S(1)} %get-tuple-element.24, f32[100]{0:T(128)S(1)} %copy-done.8, f32[16,128]{1,0:T(8,128)S(1)} %get-tuple-element.23, f32[100]{0:T(128)S(1)} %get-tuple-element.31, ...), kind=kLoop, calls=%fused_computation.86 | loop fusion | flops 4096000 | bytes 8225968 | tf_op jit(solution)/shard_map/mul | solution.py:53
  82.7 1.3 %copy.80 = f32[100,2048]{0,1:T(8,128)} copy(f32[100,2048]{1,0:T(8,128)S(1)} %convolution_bitcast_fusion.1) | data formatting | bytes 1638400 | tf_op jit(solution)/shard_map/reshape | solution.py:66
  84.0 2.3 %slice_add_fusion.15 = (f32[100,16,128]{0,2,1:T(8,128)}, f32[100,16,128]{0,2,1:T(8,128)S(1)}) fusion(f32[100,22,134]{0,2,1:T(8,128)S(1)} %fusion.22, f32[100,16,128]{0,2,1:T(8,128)} %bitcast.94, s32[16,128]{1,0:T(8,128)S(1)} %slice.445), kind=kLoop, calls=%fused_computation.82 | loop fusion | flops 614400 | bytes 3284992 | tf_op jit(solution)/shard_map/add | solution.py:110
  86.2 1.7 %copy.71 = f32[100,16,128]{2,1,0:T(8,128)S(1)} copy(f32[100,16,128]{0,2,1:T(8,128)} %get-tuple-element.2) | data formatting | bytes 1638400 | tf_op jit(solution)/shard_map/add | solution.py:110
  88.1 3.7 %convolution_bitcast_fusion.3 = f32[8,4,8,25]{3,2,1,0:T(8,128)S(1)} fusion(f32[8,8,2048,1]{2,1,3,0:T(8,128)} %convolution_bitcast_fusion.2, f32[4,25,2048,1]{2,1,0,3:T(8,128)S(1)} %reshape.93), kind=kOutput, calls=%fused_computation.81 | convolution fusion | flops 157286400 | bytes 1369088 | tf_op jit(solution)/shard_map/dot_general | solution.py:112
  92.6 3.4 %all-to-all-start.1 = ((f32[32,1,200]{2,1,0:T(1,128)}), f32[32,1,200]{2,1,0:T(1,128)S(1)}, u32[]{:S(2)}, u32[]{:S(2)}) async-start(f32[32,1,200]{2,1,0:T(1,128)} %all_to_all.25), calls=%async_computation.1 | async-start | bytes 65536 | tf_op jit(solution)/shard_map/all_to_all | solution.py:117
  96.0 1.3 %copy.69 = f32[100,16,128]{2,1,0:T(8,128)} copy(f32[100,16,128]{0,2,1:T(8,128)S(1)} %get-tuple-element.3) | data formatting | bytes 1638400 | tf_op jit(solution)/shard_map/mul | solution.py:68
  97.3 5.9 %all-to-all-done.1 = f32[32,1,200]{2,1,0:T(1,128)S(1)} async-done(((f32[32,1,200]{2,1,0:T(1,128)}), f32[32,1,200]{2,1,0:T(1,128)S(1)}, u32[]{:S(2)}, u32[]{:S(2)}) %all-to-all-start.1) | async-done | bytes 25632 | tf_op jit(solution)/shard_map/all_to_all | solution.py:117
  103.2 3.5 %all-to-all-start = ((f32[100,16,128]{2,1,0:T(8,128)}), f32[100,16,128]{2,1,0:T(8,128)S(1)}, u32[]{:S(2)}, u32[]{:S(2)}) async-start(f32[100,16,128]{2,1,0:T(8,128)} %copy.69), calls=%async_computation | async-start | bytes 1638400 | tf_op jit(solution)/shard_map/all_to_all | solution.py:111
  107.5 11.2 %all-to-all-done = f32[100,16,128]{2,1,0:T(8,128)S(1)} async-done(((f32[100,16,128]{2,1,0:T(8,128)}), f32[100,16,128]{2,1,0:T(8,128)S(1)}, u32[]{:S(2)}, u32[]{:S(2)}) %all-to-all-start) | async-done | bytes 819232 | tf_op jit(solution)/shard_map/all_to_all | solution.py:111
  (101 shorter events, 30.0 us)
Async XLA Ops:
  0.6 72.2 %copy-start = (f32[100,100]{1,0:T(8,128)S(1)}, f32[100,100]{1,0:T(8,128)}, u32[]{:S(2)}) copy-start(f32[100,100]{1,0:T(8,128)} %param.12) | copy-start | bytes 120004
  4.0 7.0 %copy-start.12 = (f32[3,100]{1,0:T(4,128)S(1)}, f32[3,100]{1,0:T(4,128)}, u32[]{:S(2)}) copy-start(f32[3,100]{1,0:T(4,128)} %param.10) | copy-start | bytes 3604
  4.0 8.3 %copy-start.13 = (s32[256]{0:T(256)S(1)}, s32[256]{0:T(256)}, u32[]{:S(2)}) copy-start(s32[256]{0:T(256)} %param.13) | copy-start | bytes 3076
  4.0 8.3 %copy-start.14 = (f32[256]{0:T(256)S(1)}, f32[256]{0:T(256)}, u32[]{:S(2)}) copy-start(f32[256]{0:T(256)} %param.15) | copy-start | bytes 3076
  4.0 8.2 %copy-start.15 = (s32[256]{0:T(256)S(1)}, s32[256]{0:T(256)}, u32[]{:S(2)}) copy-start(s32[256]{0:T(256)} %param.14) | copy-start | bytes 3076
  4.4 10.0 %collective-permute-start.1 = (f32[29,64,6]{1,0,2:T(8,128)S(1)}, f32[29,64,6]{1,0,2:T(8,128)S(1)}, u32[]{:S(2)}, u32[]{:S(2)}) collective-permute-start(f32[29,64,6]{1,0,2:T(8,128)S(1)} %copy.48), channel_id=1, source_target_pairs={{16,0},{17,1},{18,2},{19,3},{20,4},{21,5},{22,6},{23,7},{24,8},{25... | collective-permute-start | bytes 133640 | tf_op jit(solution)/shard_map/ppermute | solution.py:40
  5.7 9.1 %copy-start.1 = (f32[3,64,128]{2,1,0:T(8,128)S(1)}, f32[3,64,128]{2,1,0:T(8,128)}, u32[]{:S(2)}) copy-start(f32[3,64,128]{2,1,0:T(8,128)} %param.9) | copy-start | bytes 294916
  6.1 7.9 %collective-permute-start = (f32[29,64,6]{1,0,2:T(8,128)S(1)}, f32[29,64,6]{1,0,2:T(8,128)S(1)}, u32[]{:S(2)}, u32[]{:S(2)}) collective-permute-start(f32[29,64,6]{1,0,2:T(8,128)S(1)} %copy.47), channel_id=1, source_target_pairs={{0,16},{1,17},{2,18},{3,19},{4,20},{5,21},{6,22},{7,23},{8,24},{9,... | collective-permute-start | bytes 133640 | tf_op jit(solution)/shard_map/ppermute | solution.py:37
  15.1 9.1 %collective-permute-start.2 = (f32[29,6,140]{2,1,0:T(8,128)S(1)}, f32[29,6,140]{2,1,0:T(8,128)S(1)}, u32[]{:S(2)}, u32[]{:S(2)}) collective-permute-start(f32[29,6,140]{2,1,0:T(8,128)S(1)} %get-tuple-element.10), channel_id=1, source_target_pairs={{0,4},{4,8},{8,12},{1,5},{5,9},{9,13},{2,6},{6,10},{10,14},{3,7},{... | collective-permute-start | bytes 292328 | tf_op jit(solution)/shard_map/ppermute | solution.py:37
  19.7 8.6 %collective-permute-start.3 = (f32[29,6,140]{2,1,0:T(8,128)S(1)}, f32[29,6,140]{2,1,0:T(8,128)S(1)}, u32[]{:S(2)}, u32[]{:S(2)}) collective-permute-start(f32[29,6,140]{2,1,0:T(8,128)S(1)} %get-tuple-element.11), channel_id=1, source_target_pairs={{4,0},{8,4},{12,8},{5,1},{9,5},{13,9},{6,2},{10,6},{14,10},{7,3},{... | collective-permute-start | bytes 292328 | tf_op jit(solution)/shard_map/ppermute | solution.py:40
  28.4 0.6 copy-start.3
  38.0 0.6 copy-start.10
  38.1 0.7 copy-start.11
  42.5 0.9 copy-start.4
  51.6 2.1 %copy-start.2 = (f32[3,76,140]{2,1,0:T(8,128)S(1)}, f32[3,76,140]{2,1,0:T(8,128)}, u32[]{:S(2)}) copy-start(f32[3,76,140]{2,1,0:T(8,128)} %slice.484) | copy-start | bytes 383044
  51.8 11.4 %collective-permute-start.6 = (f32[1,25,2948]{2,1,0:T(8,128)S(1)}, f32[1,25,2948]{2,1,0:T(8,128)S(1)}, u32[]{:S(2)}, u32[]{:S(2)}) collective-permute-start(f32[1,25,2948]{2,1,0:T(8,128)S(1)} %get-tuple-element.17), channel_id=1, source_target_pairs={{0,3},{1,2},{2,1},{3,0},{4,7},{5,6},{6,5},{7,4},{8,11},{9,10},{10,... | collective-permute-start | bytes 884408 | tf_op jit(solution)/shard_map/ppermute | solution.py:28
  51.9 19.8 %collective-permute-start.5 = (f32[1,25,2948]{2,1,0:T(8,128)S(1)}, f32[1,25,2948]{2,1,0:T(8,128)S(1)}, u32[]{:S(2)}, u32[]{:S(2)}) collective-permute-start(f32[1,25,2948]{2,1,0:T(8,128)S(1)} %get-tuple-element.18), channel_id=1, source_target_pairs={{0,2},{1,3},{2,0},{3,1},{4,6},{5,7},{6,4},{7,5},{8,10},{9,11},{10,... | collective-permute-start | bytes 884408 | tf_op jit(solution)/shard_map/ppermute | solution.py:28
  53.5 18.3 %collective-permute-start.4 = (f32[1,25,2948]{2,1,0:T(8,128)S(1)}, f32[1,25,2948]{2,1,0:T(8,128)S(1)}, u32[]{:S(2)}, u32[]{:S(2)}) collective-permute-start(f32[1,25,2948]{2,1,0:T(8,128)S(1)} %get-tuple-element.19), channel_id=1, source_target_pairs={{0,1},{1,0},{2,3},{3,2},{4,5},{5,4},{6,7},{7,6},{8,9},{9,8},{10,11... | collective-permute-start | bytes 884408 | tf_op jit(solution)/shard_map/ppermute | solution.py:28
  74.6 0.7 copy-start.6
  75.3 0.7 copy-start.7
  75.3 0.7 copy-start.8
  76.1 1.9 %copy-start.5 = (s32[18,130]{1,0:T(8,128)S(1)}, s32[18,130]{1,0:T(8,128)}, u32[]{:S(2)}) copy-start(s32[18,130]{1,0:T(8,128)} %slice.446) | copy-start | bytes 28084
  92.6 10.7 %all-to-all-start.1 = ((f32[32,1,200]{2,1,0:T(1,128)}), f32[32,1,200]{2,1,0:T(1,128)S(1)}, u32[]{:S(2)}, u32[]{:S(2)}) async-start(f32[32,1,200]{2,1,0:T(1,128)} %all_to_all.25), calls=%async_computation.1 | async-start | bytes 65536 | tf_op jit(solution)/shard_map/all_to_all | solution.py:117
  103.2 15.5 %all-to-all-start = ((f32[100,16,128]{2,1,0:T(8,128)}), f32[100,16,128]{2,1,0:T(8,128)S(1)}, u32[]{:S(2)}, u32[]{:S(2)}) async-start(f32[100,16,128]{2,1,0:T(8,128)} %copy.69), calls=%async_computation | async-start | bytes 1638400 | tf_op jit(solution)/shard_map/all_to_all | solution.py:111
  (1 other events, 0.6 us)
